TPU v7x, 128 devices: a whole 4x4x4 slice. The times are simulated.
128 devices in a mesh: row: 16 (over z, y), col: 8 (over x, core).
Axes of the slice: x: 4, y: 4, z: 4, core: 2. Of those that a mesh axis runs over, the one named last changes fastest.
Arguments:
- density: float32 [8192, 8192], P('row', 'col'), may hold values from -0.63067231 to 0.63067231, as said below
- pattern_p: int32 [64, 64], replicated, may hold values from 0 to 1, as said below
- pattern_sq: int32 [64, 64], replicated, may hold values from 0 to 1, as said below
- pattern_cube: int32 [64, 64], replicated, may hold values from 0 to 1, as said below
- placement: int32 [64], replicated, may hold values from 0 to 63, each once
Outputs:
- purified: float32 [8192, 8192], P('row', 'col')
Inputs may be any that keep to these rules, and one draw needn't show every extreme that they name: density is symmetric. `pattern_p`: symmetric; every diagonal block is kept. `pattern_sq`: symmetric; every diagonal block is kept. `pattern_cube`: symmetric; every diagonal block is kept.
All inputs are finite; a program needn't handle non-finite values.
Results may differ from a plain program's by a relative error of at most 0.000058.
Values sent between devices are 32-bit elements; how exact they have to be, the bound alone decides.
A program may use at most 128 MiB of HBM per device.

v0:
```python
import jax
import jax.numpy as jnp
from jax import lax
from jax.sharding import PartitionSpec as P

BLOCK = 128


def local_mask(pattern, onehot, row_start, col_start, row_blocks, col_blocks):
    moved = jnp.dot(onehot.T, pattern.astype(jnp.float32), precision=lax.Precision.HIGHEST)
    moved = jnp.dot(moved, onehot, precision=lax.Precision.HIGHEST)
    piece = lax.dynamic_slice(moved, (row_start, col_start), (row_blocks, col_blocks))
    return jnp.repeat(jnp.repeat(piece, BLOCK, axis=0), BLOCK, axis=1)


def body(density, pattern_p, pattern_sq, pattern_cube, placement):
    count = pattern_p.shape[0]
    row_blocks = density.shape[0] // BLOCK
    col_blocks = density.shape[1] // BLOCK
    row_start = lax.axis_index("row") * row_blocks
    col_start = lax.axis_index("col") * col_blocks
    onehot = (placement[:, None] == jnp.arange(count, dtype=jnp.int32)[None, :]).astype(jnp.float32)
    kept = density * local_mask(pattern_p, onehot, row_start, col_start, row_blocks, col_blocks)
    mask_sq = local_mask(pattern_sq, onehot, row_start, col_start, row_blocks, col_blocks)
    mask_cube = local_mask(pattern_cube, onehot, row_start, col_start, row_blocks, col_blocks)
    kept_panel = lax.all_gather(kept, "col", axis=1, tiled=True)
    columns = lax.all_gather(kept, "row", axis=0, tiled=True)
    square = jnp.dot(kept_panel, columns, precision=lax.Precision.HIGHEST) * mask_sq
    square_panel = lax.all_gather(square, "col", axis=1, tiled=True)
    cube = jnp.dot(square_panel, columns, precision=lax.Precision.HIGHEST) * mask_cube
    return 3.0 * square - 2.0 * cube


def solution(mesh):
    return jax.shard_map(
        body,
        mesh=mesh,
        in_specs=(P("row", "col"), P(), P(), P(), P()),
        out_specs=P("row", "col"),
        check_vma=False,
    )
```

profile of v0, /device:TPU:0, one launch (start us, length us, event | category | flops | bytes accessed | tf_op | source)
XLA Modules:
  0.0 512.6 jit_solution(608153623267629968)
XLA Ops:
  6.5 0.0 copy-start
  6.5 0.0 all-gather.4.cloned.1.call-start
  6.5 1.2 fusion.6
  7.7 0.9 fusion.10
  8.6 0.1 dynamic_slice.9
  8.7 0.6 broadcast_in_dim.21
  9.3 0.0 copy-done
  9.3 2.0 bitcast_multiply_fusion.2
  11.4 0.0 copy-start.2
  11.4 0.0 copy-start.4
  11.4 0.0 all-gather.4.cloned.1.call-update
  11.4 0.0 all-gather.6.cloned.1.call-start
  11.4 0.7 all-gather.6.cloned.1.call-update
  12.2 0.0 all-gather.8.cloned.1.call-start
  12.2 0.0 copy-done.2
  12.2 0.0 copy-done.4
  12.2 0.3 fusion.4
  12.5 0.2 fusion.9
  12.7 0.1 dynamic_slice.10
  12.8 86.1 %all-gather.4.cloned.1.call-done = f32[512,8192]{1,0:T(8,128)} async-done(((f32[512,1024]{1,0:T(8,128)}), f32[512,8192]{1,0:T(8,128)}) %all-gather.4.cloned.1.call-update) | async-done | bytes 16777232 | tf_op jit(solution)/shard_map/all_gather | solution.py:26
  99.0 200.0 %all-gather.6.cloned.1.call-done = f32[8192,1024]{1,0:T(8,128)} async-done(((f32[512,1024]{1,0:T(8,128)}), f32[8192,1024]{1,0:T(8,128)}) %all-gather.6.cloned.1.call-update) | async-done | bytes 33554448 | tf_op jit(solution)/shard_map/all_gather | solution.py:27
  299.0 0.6 broadcast_in_dim.23
  299.6 59.9 %bitcast_multiply_fusion.1 = f32[512,1024]{1,0:T(8,128)} fusion(f32[64,8,8,128]{3,2,1,0:T(8,128)S(1)} %bitcast.25, f32[512,8192]{1,0:T(8,128)} %all-gather.4.cloned.1.call-done, f32[8192,1024]{1,0:T(8,128)} %all-gather.6.cloned.1.call-done), kind=kOutput, calls=%fused_computation.3 | convolution fusion | flops 51540131840 | bytes 54525952 | tf_op jit(solution)/shard_map/dot_general | solution.py:28
  359.5 0.0 all-gather.8.cloned.1.call-update
  359.5 0.7 copy-done.3
  360.2 0.3 fusion.2
  360.5 0.2 fusion.8
  360.7 0.1 dynamic_slice.11
  360.8 83.3 %all-gather.8.cloned.1.call-done = f32[512,8192]{1,0:T(8,128)} async-done(((f32[512,1024]{1,0:T(8,128)}), f32[512,8192]{1,0:T(8,128)}) %all-gather.8.cloned.1.call-update) | async-done | bytes 16777232 | tf_op jit(solution)/shard_map/all_gather | solution.py:29
  444.2 0.6 broadcast_in_dim.25
  444.8 0.0 copy-done.1
  444.8 61.3 %fusion.1 = f32[512,1024]{1,0:T(8,128)} fusion(f32[64,8,8,128]{3,2,1,0:T(8,128)S(1)} %bitcast.24, f32[512,1024]{1,0:T(8,128)S(1)} %copy-done.1, f32[512,8192]{1,0:T(8,128)} %all-gather.8.cloned.1.call-done, f32[8192,1024]{1,0:T(8,128)} %all-gather.6.cloned.1.call-done), kind=kOutput, calls=%fused_computation.2 | convolution fusion | flops 51541704704 | bytes 56623104 | tf_op jit(solution)/shard_map/dot_general | solution.py:30
  (5 shorter events, 0.1 us)
Async XLA Ops:
  6.5 2.8 copy-start
  6.5 92.4 %all-gather.4.cloned.1.call-start = ((), (), s32[]{:S(2)}) async-start(), calls=%async_computation | async-start | bytes 18874368 | tf_op jit(solution)/shard_map/all_gather | solution.py:26
  11.4 0.8 copy-start.2
  11.4 0.8 copy-start.4
  11.4 287.6 %all-gather.6.cloned.1.call-start = ((), (), s32[]{:S(2)}) async-start(), calls=%async_computation.1 | async-start | bytes 35651584 | tf_op jit(solution)/shard_map/all_gather | solution.py:27
  12.2 432.0 %all-gather.8.cloned.1.call-start = ((), (), s32[]{:S(2)}) async-start(), calls=%async_computation.2 | async-start | bytes 18874368 | tf_op jit(solution)/shard_map/all_gather | solution.py:29
  359.5 0.8 copy-start.3
  359.5 85.3 %copy-start.1 = (f32[512,1024]{1,0:T(8,128)S(1)}, f32[512,1024]{1,0:T(8,128)}, u32[]{:S(2)}) copy-start(f32[512,1024]{1,0:T(8,128)} %bitcast_multiply_fusion.1) | copy-start | bytes 6291460
Sparse Core Ops, SparseCore 0:
  11.5 87.3 all-gather.3
  101.1 197.8 all-gather.5
  359.6 84.4 all-gather.7
where the time goes:
time: 514 us; the launch traced here: 513 us
  waiting for transfers between devices  370 us (72%)
  matrix products  124 us (24%)
  between operations  13.2 us (3%)
    all_gather x1, waiting for transfers between devices, body(): columns = lax.all_gather(kept, 'row', axis=0, tiled=True)  200 us
    all_gather x1, waiting for transfers between devices, body(): kept_panel = lax.all_gather(kept, 'col', axis=1, tiled=True)  86.1 us
    all_gather x1, waiting for transfers between devices, body(): square_panel = lax.all_gather(square, 'col', axis=1, tiled=True)  83.3 us
    dot_general x1, matrix products, body(): jnp.dot(square_panel, columns, precision=lax.Precision.HIGHEST) * mask_cube  61.3 us
    dot_general x1, matrix products, body(): jnp.dot(kept_panel, columns, precision=lax.Precision.HIGHEST) * mask_sq  59.9 us
  transfers between devices with their start and end apart: 3, of which 3 were waited for; matrix products, arithmetic and copies ran while one was open for 0% of the time, Pallas kernels for 0%

commit v1 on v0

v1 whole, which is shorter than its diff:
```python
import functools

import jax
import jax.numpy as jnp
from jax import lax
from jax.experimental import pallas as pl
from jax.experimental.pallas import tpu as pltpu
from jax.sharding import PartitionSpec as P

BLOCK = 128
MESH = pl.DeviceIdType.MESH
CAPS = (12, 10, 9, 9)
ENDS = (12, 22, 31, 40)
STARTS = (0, 12, 22, 31)
SLOTS = 40
ZERO = tuple(8 * cap for cap in CAPS)
FIRST = 16


def local_mask(stored, row_start, col_start, row_blocks, col_blocks):
    piece = lax.dynamic_slice(stored, (row_start, col_start), (row_blocks, col_blocks))
    return jnp.repeat(jnp.repeat(piece, BLOCK, axis=0), BLOCK, axis=1)


def dense(density, stored_p, stored_sq, stored_cube):
    row_blocks = density.shape[0] // BLOCK
    col_blocks = density.shape[1] // BLOCK
    row_start = lax.axis_index("row") * row_blocks
    col_start = lax.axis_index("col") * col_blocks
    kept = density * local_mask(stored_p, row_start, col_start, row_blocks, col_blocks)
    mask_sq = local_mask(stored_sq, row_start, col_start, row_blocks, col_blocks)
    mask_cube = local_mask(stored_cube, row_start, col_start, row_blocks, col_blocks)
    kept_panel = lax.all_gather(kept, "col", axis=1, tiled=True)
    columns = lax.all_gather(kept, "row", axis=0, tiled=True)
    square = jnp.dot(kept_panel, columns, precision=lax.Precision.HIGHEST) * mask_sq
    square_panel = lax.all_gather(square, "col", axis=1, tiled=True)
    cube = jnp.dot(square_panel, columns, precision=lax.Precision.HIGHEST) * mask_cube
    return 3.0 * square - 2.0 * cube


def before(x, through=False):
    size = x.shape[-1]
    tri = jnp.arange(size)[:, None] < jnp.arange(size)[None, :] + int(through)
    sums = jnp.dot(x.astype(jnp.float32), tri.astype(jnp.float32), precision=lax.Precision.HIGHEST)
    return sums.astype(jnp.int32)


def plan(stored_p, row, col):
    z, y = row // 4, row % 4
    kept = stored_p.astype(jnp.int32)
    x = kept.reshape(4, 4, 4, 8, 4, 2).transpose(3, 0, 1, 4, 2, 5).reshape(8, 4, 4, 4, 8)
    n = x.sum(-1)
    total = before(n, True).astype(jnp.float32)
    whole = total.sum((1, 2), keepdims=True)
    by_z = total.sum(2, keepdims=True)
    by_y = total.sum(1, keepdims=True)
    even = (jnp.arange(4)[:, None] + jnp.arange(4)[None, :]) % 2
    dither = (even.astype(jnp.float32) * 0.5 + 0.25)[None, :, :, None]
    target = jnp.floor(total / 2 + (by_y - by_z) / 8 + dither).astype(jnp.int32)
    have = jnp.zeros(n.shape[:3], jnp.int32)
    incs = []
    for q in range(4):
        inc = jnp.clip(target[..., q] - have, 0, n[..., q])
        have = have + inc
        incs.append(inc)
    inc = jnp.stack(incs, -1)
    first = x * (before(x) < inc[..., None]).astype(jnp.int32)
    second = x - first
    ok = jnp.bool_(True)
    for s in (first, second):
        ok = ok & jnp.all(s.sum((3, 4)) <= FIRST)

    def ordered(s, members):
        g = s.transpose(0, 1, 3, 2, 4) if members == "y" else s.transpose(0, 2, 3, 1, 4)
        flat = g.reshape(8, 4, 4, 32)
        cnt = flat.sum(-1)
        start = jnp.zeros((8, 4), jnp.int32)
        good = jnp.bool_(True)
        starts = []
        for q in range(4):
            start = jnp.maximum(start, STARTS[max(q - 1, 0)])
            starts.append(start)
            start = start + cnt[..., q]
            good = good & jnp.all(start <= ENDS[q])
        pos = jnp.stack(starts, -1)[..., None] + before(flat)
        pos = pos.reshape(8, 4, 4, 4, 8)
        pos = pos.transpose(0, 1, 3, 2, 4) if members == "y" else pos.transpose(0, 3, 1, 2, 4)
        return pos, good

    pos0, good0 = ordered(first, "y")
    pos1, good1 = ordered(second, "z")
    ok = ok & good0 & good1

    take = lambda t: lax.dynamic_index_in_dim(t, col, 0, keepdims=False)
    first, second, pos0, pos1 = (take(t) for t in (first, second, pos0, pos1))
    at0 = before(first.reshape(4, 4, 32)).reshape(4, 4, 4, 8)
    at1 = before(second.reshape(4, 4, 32)).reshape(4, 4, 4, 8)

    ids = (
        jnp.arange(4)[:, None, None] * 2
        + jnp.arange(4)[None, :, None] * 8
        + jnp.arange(2)[None, None, :]
    ).reshape(32)
    slots = jnp.arange(FIRST)
    own = lambda t: t[z, y].reshape(32)
    pack = [
        jnp.sum(jnp.where((own(a)[None] == slots[:, None]) & (own(s)[None] > 0), ids[None], 0), -1)
        for s, a in ((first, at0), (second, at1))
    ]
    member = jnp.arange(4)[:, None, None] * FIRST
    places = jnp.arange(SLOTS)
    gather = []
    for s, a, p in (
        (first[z], at0[z], pos0[z]),
        (second[:, y], at1[:, y], pos1[:, y]),
    ):
        src = (member + a).reshape(128)
        hit = (p.reshape(128)[None] == places[:, None]) & (s.reshape(128)[None] > 0)
        gather.append(jnp.sum(jnp.where(hit, src[None], 0), -1))
    group0 = jnp.arange(4)[:, None, None, None]
    group1 = 4 + jnp.arange(4)[None, :, None, None]
    locs = []
    for q in range(4):
        f, s = first[:, :, q], second[:, :, q]
        pos = jnp.where(f > 0, pos0[:, :, q], pos1[:, :, q])
        group = jnp.where(f > 0, group0[:, :, 0], group1[:, :, 0])
        there = (f + s) > 0
        late = pos >= STARTS[q]
        cur = jnp.where(there & late, group * CAPS[q] + pos - STARTS[q], ZERO[q])
        p = max(q - 1, 0)
        prev = jnp.where(there & ~late, group * CAPS[p] + pos - STARTS[p], ZERO[p])
        locs.append(jnp.stack([prev, cur], -1).reshape(256))
    return ok, jnp.concatenate(pack), jnp.concatenate(gather), jnp.concatenate(locs)


def split(x):
    hi = x.astype(jnp.bfloat16)
    lo = (x - hi.astype(jnp.float32)).astype(jnp.bfloat16)
    return hi, lo


def product(left, right):
    lh, ll = split(left)
    rh, rl = split(right)
    lhs = jnp.concatenate([lh, lh, ll], axis=1)
    rhs = jnp.concatenate([rh, rl, rh], axis=0)
    return jnp.dot(lhs, rhs, preferred_element_type=jnp.float32)


class Ring:
    def __init__(self, part, size, me, plus, minus, ss, rs, base):
        up, down = lax.rem(me + 1, 4), lax.rem(me + 3, 4)
        cut = (size + 1) // 2
        own, left, right = part(me, 0, size), part(down, 0, size), part(up, 0, size)
        copy = lambda ref, n, dev: pltpu.make_async_remote_copy(
            src_ref=ref,
            dst_ref=ref,
            send_sem=ss.at[base + n],
            recv_sem=rs.at[base + n],
            device_id=dev,
            device_id_type=MESH,
        )
        self.copies = [
            copy(own, 0, plus),
            copy(own, 1, minus),
            copy(part(down, 0, cut), 2, plus),
            copy(part(up, cut, size - cut), 3, minus),
        ]

    def near(self):
        self.copies[0].start()
        self.copies[1].start()

    def far(self):
        self.copies[0].wait_recv()
        self.copies[2].start()
        self.copies[1].wait_recv()
        self.copies[3].start()

    def done(self):
        self.copies[2].wait_recv()
        self.copies[3].wait_recv()

    def sent(self):
        for c in self.copies:
            c.wait_send()


class Twin:
    def __init__(self, part, size, me, twin, ss, rs, base):
        self.copies = []
        for n in range(4):
            ref = part(lax.rem(me + n, 4), 0, size)
            self.copies.append(
                pltpu.make_async_remote_copy(
                    src_ref=ref,
                    dst_ref=ref,
                    send_sem=ss.at[base + n],
                    recv_sem=rs.at[base + n],
                    device_id=twin,
                    device_id_type=MESH,
                )
            )

    def start(self, *which):
        for n in which:
            self.copies[n].start()

    def recv(self, *which):
        for n in which:
            self.copies[n].wait_recv()

    def sent(self):
        for c in self.copies:
            c.wait_send()


COPIES = 8 + 8 + 4 * 8 + 4 * 8


def kernel(
    dens, pack, gather, locs, mask_p, mask_sq, mask_cube,
    out,
    a_buf, g0, g1, b0, b1, b2, b3, s2, s3, acc, ss, rs, own_sem,
):
    row, col = lax.axis_index("row"), lax.axis_index("col")
    z, y, x, core = row // 4, lax.rem(row, 4), col // 2, lax.rem(col, 2)
    up = lambda v: lax.rem(v + 1, 4)
    down = lambda v: lax.rem(v + 3, 4)
    yp, ym = (z * 4 + up(y), col), (z * 4 + down(y), col)
    zp, zm = (up(z) * 4 + y, col), (down(z) * 4 + y, col)
    xp, xm = (row, up(x) * 2 + core), (row, down(x) * 2 + core)
    twin = (row, x * 2 + 1 - core)
    pieces = (b0, b1, b2, b3)
    squares = (g0, g1, s2, s3)

    barrier = pltpu.get_barrier_semaphore()
    for dev in (yp, ym, zp, zm, xp, xm, twin):
        pl.semaphore_signal(barrier, inc=1, device_id=dev, device_id_type=MESH)

    mine = pltpu.make_async_copy(dens, a_buf.at[col], own_sem)
    mine.start()
    zero = jnp.zeros((BLOCK, BLOCK), jnp.float32)
    for piece, at in zip(pieces, ZERO):
        piece[at] = zero

    for i in range(4):
        for j in range(8):
            s2[i * 8 + j] = dens[i * BLOCK : (i + 1) * BLOCK, j * BLOCK : (j + 1) * BLOCK]

    def fill(s, _):
        g0[y * FIRST + s] = s2[pack[s]]
        g1[z * FIRST + s] = s2[pack[FIRST + s]]
        return 0

    lax.fori_loop(0, FIRST, fill, 0)
    mine.wait()

    base = 0
    a_part = lambda m, lo, n: a_buf.at[m * 2 + core, pl.ds(lo, n)]
    a_ring = Ring(a_part, 512, x, xp, xm, ss, rs, base)
    a_twin = Twin(a_part, 512, x, twin, ss, rs, base + 4)
    base += 8
    g_rings = [
        Ring(lambda m, lo, n: g0.at[pl.ds(m * FIRST + lo, n)], FIRST, y, yp, ym, ss, rs, base),
        Ring(lambda m, lo, n: g1.at[pl.ds(m * FIRST + lo, n)], FIRST, z, zp, zm, ss, rs, base + 4),
    ]
    base += 8
    b_rings = []
    for piece, cap in zip(pieces, CAPS):
        part0 = lambda m, lo, n, r=piece, c=cap: r.at[pl.ds(m * c + lo, n)]
        part1 = lambda m, lo, n, r=piece, c=cap: r.at[pl.ds((4 + m) * c + lo, n)]
        b_rings.append([
            Ring(part0, cap, z, zp, zm, ss, rs, base),
            Ring(part1, cap, y, yp, ym, ss, rs, base + 4),
        ])
        base += 8
    s_rings, s_twins = [], []
    for sq in squares:
        part = lambda m, lo, n, r=sq: r.at[pl.ds((m * 2 + core) * 8 + lo, n)]
        s_rings.append(Ring(part, 8, x, xp, xm, ss, rs, base))
        s_twins.append(Twin(part, 8, x, twin, ss, rs, base + 4))
        base += 8

    near = lambda rings: [r.near() for r in rings]
    far = lambda rings: [r.far() for r in rings]
    done = lambda rings: [r.done() for r in rings]

    pl.semaphore_wait(barrier, 7)
    near(g_rings)
    a_ring.near()
    a_twin.start(0)
    far(g_rings)
    done(g_rings)

    for q in range(4):

        def regroup(s, _, q=q):
            pieces[q][z * CAPS[q] + s] = g0[gather[STARTS[q] + s]]
            pieces[q][(4 + y) * CAPS[q] + s] = g1[gather[SLOTS + STARTS[q] + s]]
            return 0

        lax.fori_loop(0, CAPS[q], regroup, 0)
        if q < 2:
            near(b_rings[q])
    for r in g_rings:
        r.sent()

    def right_block(q, k, jj):
        at = ((q * 64 + k) * 2 + jj) * 2
        block = pieces[q][locs[at + 1]]
        if q:
            block = block + pieces[q - 1][locs[at]]
        return block

    def square(q):
        acc[...] = jnp.zeros_like(acc)

        def step(kk, _):
            k0 = kk * 4
            a = a_buf[kk // 2, :, pl.ds(pl.multiple_of(lax.rem(kk, 2) * 512, 512), 512)]
            left = jnp.concatenate([
                jnp.concatenate([
                    a[i * BLOCK : (i + 1) * BLOCK, t * BLOCK : (t + 1) * BLOCK] * mask_p[i * 64 + k0 + t]
                    for t in range(4)
                ], axis=1)
                for i in range(4)
            ], axis=0)
            right = jnp.concatenate([
                jnp.concatenate([right_block(q, k0 + t, jj) for jj in range(2)], axis=1)
                for t in range(4)
            ], axis=0)
            acc[...] += product(left, right)
            return 0

        lax.fori_loop(0, 16, step, 0)
        for i in range(4):
            for jj in range(2):
                squares[q][col * 8 + i * 2 + jj] = (
                    acc[i * BLOCK : (i + 1) * BLOCK, jj * BLOCK : (jj + 1) * BLOCK]
                    * mask_sq[i * 8 + 2 * q + jj]
                )
        s_rings[q].near()
        s_twins[q].start(0)

    def cube(q):
        def step(cd, _):
            left = jnp.concatenate([
                jnp.concatenate([squares[q][cd * 8 + i * 2 + t] for t in range(2)], axis=1)
                for i in range(4)
            ], axis=0)
            for n in range(4):
                right = jnp.concatenate([
                    jnp.concatenate([right_block(n, cd * 8 + 2 * q + t, jj) for jj in range(2)], axis=1)
                    for t in range(2)
                ], axis=0)
                out[:, n * 256 : (n + 1) * 256] += product(left, right)
            return 0

        lax.fori_loop(0, 8, step, 0)

    far(b_rings[0])
    near(b_rings[2])
    a_ring.far()
    a_twin.start(1, 3)
    done(b_rings[0])
    far(b_rings[1])
    near(b_rings[3])
    a_ring.done()
    a_twin.start(2)
    a_twin.recv(0, 1, 2, 3)
    square(0)
    done(b_rings[1])
    far(b_rings[2])
    square(1)
    s_rings[0].far()
    s_twins[0].start(1, 3)
    done(b_rings[2])
    far(b_rings[3])
    square(2)
    s_rings[0].done()
    s_twins[0].start(2)
    s_rings[1].far()
    s_twins[1].start(1, 3)
    out[...] = jnp.zeros_like(out)
    done(b_rings[3])
    square(3)
    s_rings[1].done()
    s_twins[1].start(2)
    s_rings[2].far()
    s_twins[2].start(1, 3)
    s_twins[0].recv(0, 1, 2, 3)
    cube(0)
    s_rings[2].done()
    s_twins[2].start(2)
    s_rings[3].far()
    s_twins[3].start(1, 3)
    s_twins[1].recv(0, 1, 2, 3)
    cube(1)
    s_rings[3].done()
    s_twins[3].start(2)
    s_twins[2].recv(0, 1, 2, 3)
    cube(2)
    s_twins[3].recv(0, 1, 2, 3)
    cube(3)
    for i in range(4):
        for q in range(4):
            for jj in range(2):
                j = 2 * q + jj
                at = (slice(i * BLOCK, (i + 1) * BLOCK), slice(j * BLOCK, (j + 1) * BLOCK))
                out[at] = 3.0 * squares[q][col * 8 + i * 2 + jj] - 2.0 * (out[at] * mask_cube[i * 8 + j])

    a_ring.sent()
    a_twin.sent()
    for pair in b_rings:
        for r in pair:
            r.sent()
    for r in s_rings + s_twins:
        r.sent()


def packed(density, pack, gather, locs, mask_p, mask_sq, mask_cube):
    smem = pl.BlockSpec(memory_space=pltpu.SMEM)
    vmem = pl.BlockSpec(memory_space=pltpu.VMEM)
    blocks = lambda n: pltpu.VMEM((n, BLOCK, BLOCK), jnp.float32)
    return pl.pallas_call(
        kernel,
        out_shape=jax.ShapeDtypeStruct(density.shape, jnp.float32),
        in_specs=[vmem] + [smem] * 6,
        out_specs=vmem,
        scratch_shapes=[
            pltpu.VMEM((8, 512, 1024), jnp.float32),
            blocks(64),
            blocks(64),
            *[blocks(at + 1) for at in ZERO],
            blocks(64),
            blocks(64),
            pltpu.VMEM((512, 256), jnp.float32),
            pltpu.SemaphoreType.DMA((COPIES,)),
            pltpu.SemaphoreType.DMA((COPIES,)),
            pltpu.SemaphoreType.DMA,
        ],
        compiler_params=pltpu.CompilerParams(
            collective_id=0, has_side_effects=True, vmem_limit_bytes=62 * 2**20
        ),
        cost_estimate=pl.CostEstimate(flops=6 * 2**34, bytes_accessed=2**22, transcendentals=0),
    )(density, pack, gather, locs, mask_p, mask_sq, mask_cube)


def body(density, pattern_p, pattern_sq, pattern_cube, placement):
    count = pattern_p.shape[0]
    row, col = lax.axis_index("row"), lax.axis_index("col")
    onehot = (placement[:, None] == jnp.arange(count, dtype=jnp.int32)[None, :]).astype(jnp.float32)

    def stored(pattern):
        moved = jnp.dot(onehot.T, pattern.astype(jnp.float32), precision=lax.Precision.HIGHEST)
        return jnp.dot(moved, onehot, precision=lax.Precision.HIGHEST)

    sp, ssq, scb = stored(pattern_p), stored(pattern_sq), stored(pattern_cube)
    ok, pack, gather, locs = plan(sp, row, col)
    mask_p = lax.dynamic_slice(sp, (row * 4, 0), (4, 64)).reshape(256)
    mask_sq = lax.dynamic_slice(ssq, (row * 4, col * 8), (4, 8)).reshape(32)
    mask_cube = lax.dynamic_slice(scb, (row * 4, col * 8), (4, 8)).reshape(32)
    return lax.cond(
        ok,
        lambda: packed(density, pack, gather, locs, mask_p, mask_sq, mask_cube),
        lambda: dense(density, sp, ssq, scb),
    )


def solution(mesh):
    return jax.shard_map(
        body,
        mesh=mesh,
        in_specs=(P("row", "col"), P(), P(), P(), P()),
        out_specs=P("row", "col"),
        check_vma=False,
    )
```

time: 514 us -> 243 us (0.47)
  waiting for transfers between devices: 370 us -> 0 us
  Pallas kernels: 0 us -> 198 us
  matrix products: 124 us -> 7.07 us
  local copies, waits for them, and re-layouts: 2.84 us -> 11 us
  between operations: 13.2 us -> 20.1 us
    all_gather x3 -> x0, waiting for transfers between devices: 370 us -> none  [the longest x1 200 us: body(): columns = lax.all_gather(kept, 'row', axis=0, tiled=True)]
    pallas_call x0 -> x1, Pallas kernels: none -> 198 us  [packed(): pl.pallas_call(kernel, out_shape=jax.ShapeDtypeStruct(density.shape, jnp....]
    dot_general x8 -> x12, matrix products: 124 us -> 7.07 us  [the longest x3 3.17 us: stored(): jnp.dot(onehot.T, pattern.astype(jnp.float32), precision=lax.Precision.HI...]
  transfers between devices with their start and end apart: 3 -> 0, of which waited for: 3 -> 0; matrix products, arithmetic and copies ran while one was open for 0% -> 0% of each run, Pallas kernels for 0% -> 0%
where the time goes in v1:
time: 243 us
  Pallas kernels  198 us (81%)
  between operations  20.1 us (8%)
  local copies, waits for them, and re-layouts  11 us (5%)
  matrix products  7.07 us (3%)
  other arithmetic  6.97 us (3%)
    pallas_call x1, Pallas kernels, packed(): pl.pallas_call(kernel, out_shape=jax.ShapeDtypeStruct(density.shape, jnp....  198 us

profile of v1, /device:TPU:0, one launch (start us, length us, event | category | flops | bytes accessed | tf_op | source)
XLA Modules:
  0.0 243.0 jit_solution(11807045924742960810)
XLA Ops:
  7.0 1.1 fusion.17
  8.0 1.1 fusion.14
  9.1 0.9 fusion.20
  10.0 1.1 fusion.12
  11.0 0.9 fusion.19
  11.9 0.9 fusion.77
  12.9 0.7 reshape.693
  13.5 2.3 bitcast_reduce_fusion.2
  15.8 0.2 copy.91
  16.0 0.2 fusion.70
  16.5 0.9 copy.89
  17.4 0.4 fusion.8
  17.9 0.4 bitcast_reduce_fusion.1
  18.3 0.4 bitcast_convert_fusion.1
  18.7 0.2 copy.98
  19.3 0.2 convert_reduce_fusion
  20.1 0.4 bitcast_reduce_fusion
  20.5 0.4 reduce_sum.103
  20.9 0.7 compare_reduce_fusion.12
  23.0 0.8 compare_reduce_fusion.2
  30.4 0.2 copy.100
  30.8 0.2 fusion.6
  31.8 0.2 copy.105
  32.1 0.2 copy.108
  32.4 0.2 copy.107
  32.7 0.2 copy.106
  33.1 199.9 %conditional.1 = (f32[512,1024]{1,0:T(8,128)}) conditional(s32[]{:T(128)} %convert_element_type.93, (f32[64,64]{1,0:T(8,128)S(1)}, f32[512,1024]{1,0:T(8,128)}, f32[64,64]{1,0:T(8,128)S(1)}, f32[64,64]{1,0:T(8,128)S(1)}) %tuple.11, (f32[512,1024]{1,0:T(8,128)}, s32[32]{0:T(128)S(1)}, s32[80]{0:T(128)S(1)}, s32[1024]{0:T(1024)S(1)}, ...), branch_computations={%region_21.22_spmd, %region_22.23_spmd} | conditional | flops 103082360832 | bytes 352421312 | solution.py:464
  33.5 0.6 reshape.708.mask_cube
  34.1 0.7 reshape.707.mask_sq
  34.7 0.6 reshape.706.mask_p
  35.4 197.6 %branch_1_fun.1 = f32[512,1024]{1,0:T(8,128)} custom-call(f32[512,1024]{1,0:T(8,128)} %get-tuple-element.34.dens, s32[32]{0:T(128)S(1)} %get-tuple-element.35.pack, s32[80]{0:T(128)S(1)} %get-tuple-element.36.gather, s32[1024]{0:T(1024)S(1)} %get-tuple-element.37.locs, f32[256]{0:T(256)} %reshape.706.mask_p, f32[32]{0:T(128)} %reshape.707.mask_sq, ...), custom_call_target="tpu_custom_call" | custom-call | flops 103079215104 | bytes 4194304 | tf_op jit(solution)/shard_map/cond/branch_1_fun/pallas_call | solution.py:426
  233.0 3.2 %copy.150 = f32[512,1024]{1,0:T(8,128)} copy(f32[512,1024]{1,0:T(8,128)} %get-tuple-element.41) | data formatting | bytes 4194304
  (76 shorter events, 5.1 us)

commit v2 on v1

--- a/solution.py
+++ b/solution.py
@@ -22,11 +22,19 @@
     return jnp.repeat(jnp.repeat(piece, BLOCK, axis=0), BLOCK, axis=1)
 
 
-def dense(density, stored_p, stored_sq, stored_cube):
+def dense(density, pattern_p, pattern_sq, pattern_cube, placement):
+    count = pattern_p.shape[0]
     row_blocks = density.shape[0] // BLOCK
     col_blocks = density.shape[1] // BLOCK
     row_start = lax.axis_index("row") * row_blocks
     col_start = lax.axis_index("col") * col_blocks
+    onehot = (placement[:, None] == jnp.arange(count, dtype=jnp.int32)[None, :]).astype(jnp.float32)
+
+    def stored(pattern):
+        moved = jnp.dot(onehot.T, pattern.astype(jnp.float32), precision=lax.Precision.HIGHEST)
+        return jnp.dot(moved, onehot, precision=lax.Precision.HIGHEST)
+
+    stored_p, stored_sq, stored_cube = (stored(p) for p in (pattern_p, pattern_sq, pattern_cube))
     kept = density * local_mask(stored_p, row_start, col_start, row_blocks, col_blocks)
     mask_sq = local_mask(stored_sq, row_start, col_start, row_blocks, col_blocks)
     mask_cube = local_mask(stored_cube, row_start, col_start, row_blocks, col_blocks)
@@ -38,99 +46,157 @@
     return 3.0 * square - 2.0 * cube
 
 
-def before(x, through=False):
-    size = x.shape[-1]
-    tri = jnp.arange(size)[:, None] < jnp.arange(size)[None, :] + int(through)
-    sums = jnp.dot(x.astype(jnp.float32), tri.astype(jnp.float32), precision=lax.Precision.HIGHEST)
-    return sums.astype(jnp.int32)
-
-
-def plan(stored_p, row, col):
-    z, y = row // 4, row % 4
-    kept = stored_p.astype(jnp.int32)
-    x = kept.reshape(4, 4, 4, 8, 4, 2).transpose(3, 0, 1, 4, 2, 5).reshape(8, 4, 4, 4, 8)
-    n = x.sum(-1)
-    total = before(n, True).astype(jnp.float32)
-    whole = total.sum((1, 2), keepdims=True)
-    by_z = total.sum(2, keepdims=True)
-    by_y = total.sum(1, keepdims=True)
-    even = (jnp.arange(4)[:, None] + jnp.arange(4)[None, :]) % 2
-    dither = (even.astype(jnp.float32) * 0.5 + 0.25)[None, :, :, None]
-    target = jnp.floor(total / 2 + (by_y - by_z) / 8 + dither).astype(jnp.int32)
-    have = jnp.zeros(n.shape[:3], jnp.int32)
-    incs = []
+LOC, LISTS, ROWS = 0, 64, 72
+
+
+def place():
+    return lax.axis_index("row"), lax.axis_index("col")
+
+
+def plan_kernel(where, pat_p, pat_sq, pat_cube, placement, ints, floats, fits):
+    row, col = where()
+    z, y = row // 4, lax.rem(row, 4)
+    f32, bf16 = jnp.float32, jnp.bfloat16
+
+    def grid(shape):
+        return lax.broadcasted_iota(jnp.int32, shape, 0), lax.broadcasted_iota(jnp.int32, shape, 1)
+
+    def mm(*terms):
+        out = terms[0]
+        for t in terms[1:]:
+            out = jnp.dot(out.astype(bf16), t.astype(bf16), preferred_element_type=f32)
+        return out
+
+    def one(cond):
+        return jnp.where(cond, 1.0, 0.0).astype(f32)
+
+    a, b = grid((64, 64))
+    onehot_t = one(placement[...] == a)
+
+    def stored(pattern):
+        moved = mm(onehot_t, pattern[...].astype(f32))
+        return lax.dot_general(
+            moved.astype(bf16), onehot_t.astype(bf16), (((1,), (1,)), ((), ())), preferred_element_type=f32
+        )
+
+    sp, ssq, scb = stored(pat_p), stored(pat_sq), stored(pat_cube)
+
+    d, k = grid((16, 64))
+    device_rows = one(k // 4 == d)
+    k2, d2 = grid((64, 16))
+    rows_device = one(k2 // 4 == d2)
+    j, c = grid((64, 8))
+    c2, j2 = grid((8, 64))
+    pair = [one((j // 8 == c) & (lax.rem(j, 8) // 2 == q)) for q in range(4)]
+    pair_t = [one((j2 // 8 == c2) & (lax.rem(j2, 8) // 2 == q)) for q in range(4)]
+    same_pair = one(a // 2 == b // 2)
+    pair_before = one((a // 2 == b // 2) & (a < b))
+    pairs_before = one((a // 8 == b // 8) & (a // 2 < b // 2))
+    device = a // 4 == b // 4
+    rows_before = one(device & (b < a))
+    rows_device_all = one(device)
+    d3, d4 = grid((16, 16))
+    mean = (one(lax.rem(d3, 4) == lax.rem(d4, 4)) - one(d3 // 4 == d4 // 4)) * 0.125
+    dd, _ = grid((16, 8))
+    dither = (lax.rem(dd // 4 + lax.rem(dd, 4), 2)).astype(f32) * 0.5 + 0.25
+
+    by_device = mm(device_rows, sp)
+    total = jnp.zeros((16, 8), f32)
+    have = jnp.zeros((16, 8), f32)
+    share = jnp.zeros((64, 64), f32)
     for q in range(4):
-        inc = jnp.clip(target[..., q] - have, 0, n[..., q])
+        n = mm(by_device, pair[q])
+        total = total + n
+        target = jnp.floor(total * 0.5 + mm(mean, total) + dither)
+        inc = jnp.minimum(jnp.maximum(target - have, 0.0), n)
         have = have + inc
-        incs.append(inc)
-    inc = jnp.stack(incs, -1)
-    first = x * (before(x) < inc[..., None]).astype(jnp.int32)
-    second = x - first
-    ok = jnp.bool_(True)
-    for s in (first, second):
-        ok = ok & jnp.all(s.sum((3, 4)) <= FIRST)
-
-    def ordered(s, members):
-        g = s.transpose(0, 1, 3, 2, 4) if members == "y" else s.transpose(0, 2, 3, 1, 4)
-        flat = g.reshape(8, 4, 4, 32)
-        cnt = flat.sum(-1)
-        start = jnp.zeros((8, 4), jnp.int32)
-        good = jnp.bool_(True)
-        starts = []
+        share = share + mm(mm(rows_device, inc), pair_t[q])
+    rest = total - have
+    worst = jnp.maximum(jnp.max(have - FIRST), jnp.max(rest - FIRST))
+
+    rank = mm(mm(rows_before, sp), same_pair) + mm(sp, pair_before)
+    first = sp * one(rank < share)
+    second = sp - first
+
+    routes = []
+    for sel, group_of in ((first, lambda r: r // 16), (second, lambda r: lax.rem(r // 4, 4))):
+        g, kk = grid((8, 64))
+        group_rows = one(group_of(kk) == g)
+        kk2, g2 = grid((64, 8))
+        rows_group = one(group_of(kk2) == g2)
+        by_group = mm(group_rows, sel)
+        start = jnp.zeros((8, 8), f32)
+        base = jnp.zeros((64, 64), f32)
         for q in range(4):
-            start = jnp.maximum(start, STARTS[max(q - 1, 0)])
-            starts.append(start)
-            start = start + cnt[..., q]
-            good = good & jnp.all(start <= ENDS[q])
-        pos = jnp.stack(starts, -1)[..., None] + before(flat)
-        pos = pos.reshape(8, 4, 4, 4, 8)
-        pos = pos.transpose(0, 1, 3, 2, 4) if members == "y" else pos.transpose(0, 3, 1, 2, 4)
-        return pos, good
-
-    pos0, good0 = ordered(first, "y")
-    pos1, good1 = ordered(second, "z")
-    ok = ok & good0 & good1
-
-    take = lambda t: lax.dynamic_index_in_dim(t, col, 0, keepdims=False)
-    first, second, pos0, pos1 = (take(t) for t in (first, second, pos0, pos1))
-    at0 = before(first.reshape(4, 4, 32)).reshape(4, 4, 4, 8)
-    at1 = before(second.reshape(4, 4, 32)).reshape(4, 4, 4, 8)
-
-    ids = (
-        jnp.arange(4)[:, None, None] * 2
-        + jnp.arange(4)[None, :, None] * 8
-        + jnp.arange(2)[None, None, :]
-    ).reshape(32)
-    slots = jnp.arange(FIRST)
-    own = lambda t: t[z, y].reshape(32)
-    pack = [
-        jnp.sum(jnp.where((own(a)[None] == slots[:, None]) & (own(s)[None] > 0), ids[None], 0), -1)
-        for s, a in ((first, at0), (second, at1))
-    ]
-    member = jnp.arange(4)[:, None, None] * FIRST
-    places = jnp.arange(SLOTS)
-    gather = []
-    for s, a, p in (
-        (first[z], at0[z], pos0[z]),
-        (second[:, y], at1[:, y], pos1[:, y]),
-    ):
-        src = (member + a).reshape(128)
-        hit = (p.reshape(128)[None] == places[:, None]) & (s.reshape(128)[None] > 0)
-        gather.append(jnp.sum(jnp.where(hit, src[None], 0), -1))
-    group0 = jnp.arange(4)[:, None, None, None]
-    group1 = 4 + jnp.arange(4)[None, :, None, None]
-    locs = []
-    for q in range(4):
-        f, s = first[:, :, q], second[:, :, q]
-        pos = jnp.where(f > 0, pos0[:, :, q], pos1[:, :, q])
-        group = jnp.where(f > 0, group0[:, :, 0], group1[:, :, 0])
-        there = (f + s) > 0
-        late = pos >= STARTS[q]
-        cur = jnp.where(there & late, group * CAPS[q] + pos - STARTS[q], ZERO[q])
-        p = max(q - 1, 0)
-        prev = jnp.where(there & ~late, group * CAPS[p] + pos - STARTS[p], ZERO[p])
-        locs.append(jnp.stack([prev, cur], -1).reshape(256))
-    return ok, jnp.concatenate(pack), jnp.concatenate(gather), jnp.concatenate(locs)
+            start = jnp.maximum(start, float(STARTS[max(q - 1, 0)]))
+            base = base + mm(mm(rows_group, start), pair_t[q])
+            start = start + mm(by_group, pair[q])
+            worst = jnp.maximum(worst, jnp.max(start - ENDS[q]))
+        order = one((group_of(a) == group_of(b)) & (b < a))
+        in_pair = mm(sel, pair_before)
+        pos = base + mm(mm(order, sel), same_pair) + in_pair
+        slot = mm(mm(rows_device_all, sel), pairs_before) + mm(mm(rows_before, sel), same_pair) + in_pair
+        routes.append((pos, slot))
+    fits[0, 0] = jnp.where(worst <= 0.0, 1, 0)
+
+    mine = one((j // 8 == col) & (lax.rem(j, 8) == c))
+    panel = lambda t: mm(t, mine).astype(jnp.int32)
+    sel0, sel1 = panel(first), panel(second)
+    pos0, pos1 = panel(routes[0][0]), panel(routes[1][0])
+    slot0, slot1 = panel(routes[0][1]), panel(routes[1][1])
+    r, jl = grid((64, 8))
+    pos = jnp.where(sel0 > 0, pos0, pos1)
+    group = jnp.where(sel0 > 0, r // 16, 4 + lax.rem(r // 4, 4))
+    there = (sel0 + sel1) > 0
+    q = jl // 2
+    table = lambda values: sum(jnp.where(q == n, v, 0) for n, v in enumerate(values))
+    early = tuple(max(n - 1, 0) for n in range(4))
+    late = pos >= table(STARTS)
+    cur = jnp.where(there & late, group * table(CAPS) + pos - table(STARTS), table(ZERO))
+    prev_caps = table([CAPS[p] for p in early])
+    prev_start = table([STARTS[p] for p in early])
+    prev_zero = table([ZERO[p] for p in early])
+    prev = jnp.where(there & ~late, group * prev_caps + pos - prev_start, prev_zero)
+    ints[LOC : LOC + 64, 0:8] = prev
+    ints[LOC : LOC + 64, 8:16] = cur
+
+    rr, lane = grid((64, 128))
+    ids = lax.rem(rr, 4) * 8
+    lists = [jnp.zeros((64, 128), jnp.int32) for _ in range(4)]
+    for n in range(8):
+        column = lambda t: t[:, n : n + 1]
+        for h, (sel, p, s, in_group, member) in enumerate((
+            (sel0, pos0, slot0, rr // 16 == z, lax.rem(rr // 4, 4)),
+            (sel1, pos1, slot1, lax.rem(rr // 4, 4) == y, rr // 16),
+        )):
+            on = column(sel) > 0
+            here = on & in_group & (column(p) == lane)
+            lists[h] = lists[h] + jnp.where(here, member * FIRST + column(s), 0)
+            here = on & (rr // 4 == row) & (column(s) == lane)
+            lists[2 + h] = lists[2 + h] + jnp.where(here, ids + n, 0)
+    for n, t in enumerate(lists):
+        ints[LISTS + n : LISTS + n + 1, :] = jnp.sum(t, axis=0, keepdims=True)
+
+    i8, k8 = grid((8, 64))
+    my_rows = one((k8 == row * 4 + i8) & (i8 < 4))
+    floats[0:8, 0:64] = mm(my_rows, sp)
+    floats[8:16, 0:8] = mm(mm(my_rows, ssq), mine)
+    floats[16:24, 0:8] = mm(mm(my_rows, scb), mine)
+
+
+def make_plan(pattern_p, pattern_sq, pattern_cube, placement, where=place, interpret=False):
+    vmem = pl.BlockSpec(memory_space=pltpu.VMEM)
+    return pl.pallas_call(
+        functools.partial(plan_kernel, where),
+        out_shape=(
+            jax.ShapeDtypeStruct((ROWS, 128), jnp.int32),
+            jax.ShapeDtypeStruct((24, 128), jnp.float32),
+            jax.ShapeDtypeStruct((1, 1), jnp.int32),
+        ),
+        in_specs=[vmem] * 4,
+        out_specs=(vmem, vmem, pl.BlockSpec(memory_space=pltpu.SMEM)),
+        interpret=interpret,
+    )(pattern_p, pattern_sq, pattern_cube, placement.reshape(1, 64))
 
 
 def split(x):
@@ -219,7 +285,7 @@
 
 
 def kernel(
-    dens, pack, gather, locs, mask_p, mask_sq, mask_cube,
+    dens, ints, floats,
     out,
     a_buf, g0, g1, b0, b1, b2, b3, s2, s3, acc, ss, rs, own_sem,
 ):
@@ -249,8 +315,8 @@
             s2[i * 8 + j] = dens[i * BLOCK : (i + 1) * BLOCK, j * BLOCK : (j + 1) * BLOCK]
 
     def fill(s, _):
-        g0[y * FIRST + s] = s2[pack[s]]
-        g1[z * FIRST + s] = s2[pack[FIRST + s]]
+        g0[y * FIRST + s] = s2[ints[LISTS + 2, s]]
+        g1[z * FIRST + s] = s2[ints[LISTS + 3, s]]
         return 0
 
     lax.fori_loop(0, FIRST, fill, 0)
@@ -296,8 +362,8 @@
     for q in range(4):
 
         def regroup(s, _, q=q):
-            pieces[q][z * CAPS[q] + s] = g0[gather[STARTS[q] + s]]
-            pieces[q][(4 + y) * CAPS[q] + s] = g1[gather[SLOTS + STARTS[q] + s]]
+            pieces[q][z * CAPS[q] + s] = g0[ints[LISTS, STARTS[q] + s]]
+            pieces[q][(4 + y) * CAPS[q] + s] = g1[ints[LISTS + 1, STARTS[q] + s]]
             return 0
 
         lax.fori_loop(0, CAPS[q], regroup, 0)
@@ -307,10 +373,9 @@
         r.sent()
 
     def right_block(q, k, jj):
-        at = ((q * 64 + k) * 2 + jj) * 2
-        block = pieces[q][locs[at + 1]]
+        block = pieces[q][ints[LOC + k, 8 + 2 * q + jj]]
         if q:
-            block = block + pieces[q - 1][locs[at]]
+            block = block + pieces[q - 1][ints[LOC + k, 2 * q + jj]]
         return block
 
     def square(q):
@@ -321,7 +386,7 @@
             a = a_buf[kk // 2, :, pl.ds(pl.multiple_of(lax.rem(kk, 2) * 512, 512), 512)]
             left = jnp.concatenate([
                 jnp.concatenate([
-                    a[i * BLOCK : (i + 1) * BLOCK, t * BLOCK : (t + 1) * BLOCK] * mask_p[i * 64 + k0 + t]
+                    a[i * BLOCK : (i + 1) * BLOCK, t * BLOCK : (t + 1) * BLOCK] * floats[i, k0 + t]
                     for t in range(4)
                 ], axis=1)
                 for i in range(4)
@@ -338,7 +403,7 @@
             for jj in range(2):
                 squares[q][col * 8 + i * 2 + jj] = (
                     acc[i * BLOCK : (i + 1) * BLOCK, jj * BLOCK : (jj + 1) * BLOCK]
-                    * mask_sq[i * 8 + 2 * q + jj]
+                    * floats[8 + i, 2 * q + jj]
                 )
         s_rings[q].near()
         s_twins[q].start(0)
@@ -408,7 +473,7 @@
             for jj in range(2):
                 j = 2 * q + jj
                 at = (slice(i * BLOCK, (i + 1) * BLOCK), slice(j * BLOCK, (j + 1) * BLOCK))
-                out[at] = 3.0 * squares[q][col * 8 + i * 2 + jj] - 2.0 * (out[at] * mask_cube[i * 8 + j])
+                out[at] = 3.0 * squares[q][col * 8 + i * 2 + jj] - 2.0 * (out[at] * floats[16 + i, j])
 
     a_ring.sent()
     a_twin.sent()
@@ -419,14 +484,14 @@
         r.sent()
 
 
-def packed(density, pack, gather, locs, mask_p, mask_sq, mask_cube):
+def packed(density, ints, floats):
     smem = pl.BlockSpec(memory_space=pltpu.SMEM)
     vmem = pl.BlockSpec(memory_space=pltpu.VMEM)
     blocks = lambda n: pltpu.VMEM((n, BLOCK, BLOCK), jnp.float32)
     return pl.pallas_call(
         kernel,
         out_shape=jax.ShapeDtypeStruct(density.shape, jnp.float32),
-        in_specs=[vmem] + [smem] * 6,
+        in_specs=[vmem, smem, smem],
         out_specs=vmem,
         scratch_shapes=[
             pltpu.VMEM((8, 512, 1024), jnp.float32),
@@ -444,27 +509,15 @@
             collective_id=0, has_side_effects=True, vmem_limit_bytes=62 * 2**20
         ),
         cost_estimate=pl.CostEstimate(flops=6 * 2**34, bytes_accessed=2**22, transcendentals=0),
-    )(density, pack, gather, locs, mask_p, mask_sq, mask_cube)
+    )(density, ints, floats)
 
 
 def body(density, pattern_p, pattern_sq, pattern_cube, placement):
-    count = pattern_p.shape[0]
-    row, col = lax.axis_index("row"), lax.axis_index("col")
-    onehot = (placement[:, None] == jnp.arange(count, dtype=jnp.int32)[None, :]).astype(jnp.float32)
-
-    def stored(pattern):
-        moved = jnp.dot(onehot.T, pattern.astype(jnp.float32), precision=lax.Precision.HIGHEST)
-        return jnp.dot(moved, onehot, precision=lax.Precision.HIGHEST)
-
-    sp, ssq, scb = stored(pattern_p), stored(pattern_sq), stored(pattern_cube)
-    ok, pack, gather, locs = plan(sp, row, col)
-    mask_p = lax.dynamic_slice(sp, (row * 4, 0), (4, 64)).reshape(256)
-    mask_sq = lax.dynamic_slice(ssq, (row * 4, col * 8), (4, 8)).reshape(32)
-    mask_cube = lax.dynamic_slice(scb, (row * 4, col * 8), (4, 8)).reshape(32)
+    ints, floats, fits = make_plan(pattern_p, pattern_sq, pattern_cube, placement)
     return lax.cond(
-        ok,
-        lambda: packed(density, pack, gather, locs, mask_p, mask_sq, mask_cube),
-        lambda: dense(density, sp, ssq, scb),
+        fits[0, 0] > 0,
+        lambda: packed(density, ints, floats),
+        lambda: dense(density, pattern_p, pattern_sq, pattern_cube, placement),
     )
 
 

time: 243 us -> 220 us (0.905)
  local copies, waits for them, and re-layouts: 11 us -> 3.16 us
  matrix products: 7.07 us -> 0 us
  other arithmetic: 6.97 us -> 0 us
  between operations: 20.1 us -> 14 us
  Pallas kernels: 198 us -> 202 us
    dot_general x12 -> x0, matrix products: 7.07 us -> none  [the longest x3 3.17 us: stored(): jnp.dot(onehot.T, pattern.astype(jnp.float32), precision=lax.Precision.HI...]
    pallas_call x0 -> x1, Pallas kernels: none -> 4.37 us  [make_plan(): pl.pallas_call(functools.partial(plan_kernel, where), out_shape=(jax.Shap...]
    reshape x13 -> x0, local copies, waits for them, and re-layouts: 3.75 us -> none  [the longest x2 0.78 us: plan(): kept.reshape(4, 4, 4, 8, 4, 2).transpose(3, 0, 1, 4, 2, 5)]
    reduce_sum x7 -> x0, other arithmetic: 3.73 us -> none  [the longest x1 2.29 us: plan(): n = x.sum(-1)]
where the time goes in v2:
time: 220 us; the launch traced here: 219 us
  Pallas kernels  202 us (92%)
  between operations  14 us (6%)
  local copies, waits for them, and re-layouts  3.16 us (1%)
    pallas_call x1, Pallas kernels, packed(): pl.pallas_call(kernel, out_shape=jax.ShapeDtypeStruct(density.shape, jnp....  198 us

profile of v2, /device:TPU:0, one launch (start us, length us, event | category | flops | bytes accessed | tf_op | source)
XLA Modules:
  0.0 219.3 jit_solution(17484056536422239113)
XLA Ops:
  6.5 4.4 %shard_map.57 = (s32[72,128]{1,0:T(8,128)S(1)}, f32[24,128]{1,0:T(8,128)S(1)}, s32[1,1]{1,0:T(1,128)}) custom-call(s32[64,64]{1,0:T(8,128)} %pat_p.1, s32[64,64]{1,0:T(8,128)} %pat_sq.1, s32[64,64]{1,0:T(8,128)} %pat_cube.1, s32[1,64]{1,0:T(1,128)} %bitcast.31), custom_call_target="tpu_custom_call" | custom-call | tf_op jit(solution)/shard_map/pallas_call | solution.py:189
  11.6 197.8 %conditional.1 = (f32[512,1024]{1,0:T(8,128)}) conditional(s32[]{:T(128)} %bitcast.4, (s32[64]{0:T(128)}, s32[64,64]{1,0:T(8,128)}, f32[512,1024]{1,0:T(8,128)}, s32[64,64]{1,0:T(8,128)}, s32[64,64]{1,0:T(8,128)}) %tuple.11, (f32[512,1024]{1,0:T(8,128)}, s32[72,128]{1,0:T(8,128)S(1)}, f32[24,128]{1,0:T(8,128)S(1)}) %tuple.12), branch_computations={%region_0.0_spmd, %region_1.0_spmd} | conditional | flops 103101267968 | bytes 361140224 | solution.py:517
  11.8 197.5 %branch_1_fun.1 = f32[512,1024]{1,0:T(8,128)} custom-call(f32[512,1024]{1,0:T(8,128)} %get-tuple-element.29.dens, s32[72,128]{1,0:T(8,128)S(1)} %get-tuple-element.30.ints, f32[24,128]{1,0:T(8,128)S(1)} %get-tuple-element.31.floats), custom_call_target="tpu_custom_call" | custom-call | flops 103079215104 | bytes 4194304 | tf_op jit(solution)/shard_map/cond/branch_1_fun/pallas_call | solution.py:491
  209.3 3.2 %copy.17 = f32[512,1024]{1,0:T(8,128)} copy(f32[512,1024]{1,0:T(8,128)} %get-tuple-element.38) | data formatting | bytes 4194304
